TPU v7x, 32 devices: a whole 2x2x4 slice. The times are simulated.
32 devices in a mesh: req: 4 (over x, core), tp: 8 (over z, y).
Axes of the slice: x: 2, y: 2, z: 4, core: 2. Of those that a mesh axis runs over, the one named last changes fastest.
Arguments:
- hidden: bfloat16 [4, 320, 5120], P('req'), may hold values from -6 to 6
- norm_gain: float32 [5120], replicated, may hold values from 0.5 to 2
- q_weight: float32 [5120, 1024], P(('req', 'tp')), may hold values from -0.078125 to 0.078125
- k_weight: float32 [5120, 1024], P(('req', 'tp')), may hold values from -0.078125 to 0.078125
- v_weight: float32 [5120, 1024], P(('req', 'tp')), may hold values from -0.078125 to 0.078125
- o_weight: float32 [5120, 1024], P(('req', 'tp')), may hold values from -0.5 to 0.5
- key_cache: bfloat16 [4, 512, 1024], P('req', None, 'tp'), may hold values from -160 to 160
- value_cache: bfloat16 [4, 512, 1024], P('req', None, 'tp'), may hold values from -6 to 6
- text_rows: bfloat16 [4, 256, 5120], P('req', 'tp'), may hold values from -6 to 6
- text_index: int32 [4, 256], P('req'), may hold values from 0 to 511, as said below
- clip_len: int32 [4], P('req'), may hold values from 80 to 320, as said below
- text_len: int32 [4], P('req'), may hold values from 128 to 512, as said below
Outputs:
- output: bfloat16 [4, 320, 5120], P('req', 'tp')
Inputs may be any that keep to these rules, and one draw needn't show every extreme that they name: `text_index`: within a clip the entries are distinct text rows; clip 0 always recomputes rows 0 and 511. `clip_len`: some clip has exactly 320 live slots and some clip exactly 80. `text_len`: some clip has all 512 text rows live and some clip exactly 128.
All inputs are finite; a program needn't handle non-finite values.
Results may differ from a plain program's by a relative error of at most 0.012.
The roundings to bfloat16 on the way count: a program that leaves them out, or rounds other values in their place, can miss the bound.
Values may be sent and summed in bfloat16 or wider, within the bound.
A program may use at most 64 MiB of HBM per device.

v0:
```python
import math

import jax
import jax.numpy as jnp
from jax import lax
from jax.sharding import PartitionSpec as P


def on_device(
    hidden,
    norm_gain,
    q_weight,
    k_weight,
    v_weight,
    o_weight,
    key_cache,
    value_cache,
    text_rows,
    text_index,
    clip_len,
    text_len,
):
    head_width = key_cache.shape[2]
    text_total = key_cache.shape[1]
    q_half = q_weight.astype(jnp.bfloat16)
    k_half = k_weight.astype(jnp.bfloat16)
    v_half = v_weight.astype(jnp.bfloat16)
    o_half = o_weight.astype(jnp.bfloat16)
    q_block, k_block, v_block, o_block = (
        lax.all_to_all(q_half, "tp", split_axis=1, concat_axis=0, tiled=True),
        lax.all_to_all(k_half, "tp", split_axis=1, concat_axis=0, tiled=True),
        lax.all_to_all(v_half, "tp", split_axis=1, concat_axis=0, tiled=True),
        lax.all_to_all(o_half, "tp", split_axis=1, concat_axis=0, tiled=True),
    )
    q_local, k_local, v_local, o_local = (
        lax.all_gather(q_block, "req", axis=0, tiled=True),
        lax.all_gather(k_block, "req", axis=0, tiled=True),
        lax.all_gather(v_block, "req", axis=0, tiled=True),
        lax.all_gather(o_block, "req", axis=0, tiled=True),
    )
    x32 = hidden[0].astype(jnp.float32)
    mean = jnp.mean(x32, axis=-1, keepdims=True)
    centered = x32 - mean
    var = jnp.mean(centered * centered, axis=-1, keepdims=True)
    normed = (centered * lax.rsqrt(var + 1e-06) * norm_gain).astype(jnp.bfloat16)
    kv_local = jnp.concatenate([k_local, v_local], axis=1)
    new_kv = jnp.einsum(
        "crd,de->cre",
        lax.all_gather(text_rows, "tp", axis=1, tiled=True),
        kv_local,
        preferred_element_type=jnp.float32,
    ).astype(jnp.bfloat16)
    query = jnp.dot(normed, q_local, preferred_element_type=jnp.float32).astype(jnp.bfloat16)
    selector = text_index[0][None, :] == jnp.arange(text_total, dtype=jnp.int32)[:, None]
    covered = jnp.any(selector, axis=1)
    placed = jnp.dot(
        selector.astype(jnp.bfloat16), new_kv[0], preferred_element_type=jnp.float32
    ).astype(jnp.bfloat16)
    keys = jnp.where(covered[:, None], placed[:, :head_width], key_cache[0])
    values = jnp.where(covered[:, None], placed[:, head_width:], value_cache[0])
    score = lax.dot_general(
        query, keys, (((1,), (1,)), ((), ())), preferred_element_type=jnp.float32
    ) * (1.0 / math.sqrt(head_width))
    valid = jnp.arange(text_total, dtype=jnp.int32) < text_len[0]
    score = jnp.where(valid[None, :], score, -1e30)
    top = jnp.max(score, axis=-1, keepdims=True)
    expo = jnp.exp(score - top)
    weights = (expo / jnp.sum(expo, axis=-1, keepdims=True)).astype(jnp.bfloat16)
    attended = jnp.dot(weights, values, preferred_element_type=jnp.float32).astype(jnp.bfloat16)
    tp_count = lax.axis_size("tp")
    local_rows = hidden.shape[1] // tp_count
    first_row = lax.axis_index("tp") * local_rows
    summed = lax.psum_scatter(
        lax.dot_general(
            attended, o_local, (((1,), (1,)), ((), ())), preferred_element_type=jnp.float32
        ).astype(jnp.bfloat16),
        "tp",
        scatter_dimension=0,
        tiled=True,
    ).astype(jnp.float32)
    own_rows = lax.dynamic_slice_in_dim(x32, first_row, local_rows, 0)
    positions = first_row + jnp.arange(local_rows, dtype=jnp.int32)
    live = positions < clip_len[0]
    result = own_rows + jnp.where(live[:, None], summed, 0.0)
    return result.astype(jnp.bfloat16)[None]


def solution(mesh):
    return jax.shard_map(
        on_device,
        mesh=mesh,
        in_specs=(
            P("req", None, None),
            P(),
            P(("req", "tp"), None),
            P(("req", "tp"), None),
            P(("req", "tp"), None),
            P(("req", "tp"), None),
            P("req", None, "tp"),
            P("req", None, "tp"),
            P("req", "tp", None),
            P("req", None),
            P("req"),
            P("req"),
        ),
        out_specs=P("req", "tp", None),
        check_vma=False,
    )
```

profile of v0, /device:TPU:0, one launch (start us, length us, event | category | flops | bytes accessed | tf_op | source)
XLA Modules:
  0.0 247.2 jit_solution(8818809206935015885)
XLA Ops:
  6.5 0.0 all-gather.8.cloned.1.call-start
  6.5 1.1 copy_bitcast_fusion.2
  7.7 18.1 %all_to_all.76 = bf16[160,8,128]{2,0,1:T(8,128)(2,1)} all-to-all(bf16[160,8,128]{2,0,1:T(8,128)(2,1)S(1)} %copy_bitcast_fusion.2), channel_id=1, replica_groups=mesh['req'=4,'tp'=8] {'tp'}, dimensions={1} | all-to-all | bytes 655360 | tf_op jit(solution)/shard_map/all_to_all | solution.py:31
  25.8 0.0 copy-start
  25.8 0.0 all-gather.8.cloned.1.call-update
  25.8 0.0 all-gather.10.cloned.1.call-start
  25.8 1.3 copy_bitcast_fusion.1
  27.1 13.7 %all_to_all.77 = bf16[160,8,128]{2,0,1:T(8,128)(2,1)} all-to-all(bf16[160,8,128]{2,0,1:T(8,128)(2,1)S(1)} %copy_bitcast_fusion.1), channel_id=1, replica_groups=mesh['req'=4,'tp'=8] {'tp'}, dimensions={1} | all-to-all | bytes 655360 | tf_op jit(solution)/shard_map/all_to_all | solution.py:32
  40.8 0.0 all-gather.10.cloned.1.call-update
  40.9 0.0 all-gather.12.cloned.1.call-start
  40.9 0.7 all-gather.12.cloned.1.call-update
  41.6 0.0 all-gather.6.cloned.1.call-start
  41.7 1.1 copy_bitcast_fusion.3
  42.8 0.0 copy-start.3
  42.8 13.2 %all_to_all.78 = bf16[160,8,128]{2,0,1:T(8,128)(2,1)} all-to-all(bf16[160,8,128]{2,0,1:T(8,128)(2,1)S(1)} %copy_bitcast_fusion.3), channel_id=1, replica_groups=mesh['req'=4,'tp'=8] {'tp'}, dimensions={1} | all-to-all | bytes 655360 | tf_op jit(solution)/shard_map/all_to_all | solution.py:30
  56.0 0.0 all-gather.6.cloned.1.call-update
  56.1 1.9 copy_bitcast_fusion
  57.9 4.1 %all-to-all-start.3 = ((bf16[160,8,128]{2,0,1:T(8,128)(2,1)}), bf16[160,8,128]{2,0,1:T(8,128)(2,1)}, u32[]{:S(2)}, u32[]{:S(2)}) async-start(bf16[160,8,128]{2,0,1:T(8,128)(2,1)} %copy_bitcast_fusion), calls=%async_computation.3 | async-start | bytes 655360 | tf_op jit(solution)/shard_map/all_to_all | solution.py:33
  62.0 0.0 all-gather.14.cloned.1.call-start
  62.7 0.0 copy-done
  62.7 0.5 convert_reduce_fusion
  63.3 7.6 %all-to-all-done.3 = bf16[160,8,128]{2,0,1:T(8,128)(2,1)} async-done(((bf16[160,8,128]{2,0,1:T(8,128)(2,1)}), bf16[160,8,128]{2,0,1:T(8,128)(2,1)}, u32[]{:S(2)}, u32[]{:S(2)}) %all-to-all-start.3) | async-done | bytes 327712 | tf_op jit(solution)/shard_map/all_to_all | solution.py:33
  70.8 0.0 all-gather.14.cloned.1.call-update
  70.9 0.0 reduce-scatter.2.cloned.1.call-start
  70.9 0.6 iota_compare_fusion.2
  71.5 0.0 copy-done.3
  71.5 0.2 fusion.22
  71.7 1.0 multiply_reduce_fusion
  72.7 0.0 copy-start.2
  72.7 0.0 all-gather.8.cloned.1.call-done
  72.7 0.0 all-gather.10.cloned.1.call-done
  72.8 46.5 %all-gather.12.cloned.1.call-done = bf16[1,256,5120]{2,1,0:T(8,128)(2,1)} async-done(((bf16[1,32,5120]{2,1,0:T(8,128)(2,1)}), bf16[1,256,5120]{2,1,0:T(8,128)(2,1)}) %all-gather.12.cloned.1.call-update) | async-done | bytes 2621456 | tf_op jit(solution)/shard_map/all_gather | solution.py:49
  119.2 4.4 %convolution_convert_fusion.1 = bf16[512,256]{1,0:T(8,128)(2,1)} fusion(bf16[1,256,5120]{2,1,0:T(8,128)(2,1)} %all-gather.12.cloned.1.call-done, bf16[5120,128]{1,0:T(8,128)(2,1)} %all-gather.10.cloned.1.call-done, bf16[5120,128]{1,0:T(8,128)(2,1)} %all-gather.8.cloned.1.call-done, s32[256]{0:T(256)S(1)} %bitcast.84), kind=kOutput, calls=%fused_computation.16 | convolution fusion | flops 743768064 | bytes 5506048 | tf_op jit(solution)/shard_map/dot_general | solution.py:56
  123.7 0.0 copy-start.1
  123.7 13.8 %all-gather.6.cloned.1.call-done = bf16[5120,128]{1,0:T(8,128)(2,1)} async-done(((bf16[1280,128]{1,0:T(8,128)(2,1)}), bf16[5120,128]{1,0:T(8,128)(2,1)}) %all-gather.6.cloned.1.call-update) | async-done | bytes 1310736 | tf_op jit(solution)/shard_map/all_gather | solution.py:36
  137.4 0.0 copy-done.2
  137.4 3.6 %fusion.37 = (f32[320]{0:T(512)S(1)}, f32[320,512]{1,0:T(8,128)}) fusion(bf16[512,256]{1,0:T(8,128)(2,1)} %convolution_convert_fusion.1, bf16[1,512,128]{2,1,0:T(8,128)(2,1)S(1)} %copy-done.2, pred[512]{0:T(512)(128)(4,1)S(1)} %fusion.22, bf16[5120,128]{1,0:T(8,128)(2,1)} %all-gather.6.cloned.1.call-done, bf16[1,320,5120]{2,1,0:T(8,128)(2,1)S(1)} %copy-done, ...), kind=kOutput, calls=%fused_computation.50 | convolution fusion | flops 470163136 | bytes 5530368 | tf_op jit(solution)/shard_map/dot_general | solution.py:61
  141.1 1.3 fusion.21
  142.4 14.7 %all-gather.14.cloned.1.call-done = bf16[5120,128]{1,0:T(8,128)(2,1)} async-done(((bf16[1280,128]{1,0:T(8,128)(2,1)}), bf16[5120,128]{1,0:T(8,128)(2,1)}) %all-gather.14.cloned.1.call-update) | async-done | bytes 1310736 | tf_op jit(solution)/shard_map/all_gather | solution.py:39
  157.1 0.0 copy-done.1
  157.1 4.8 %convolution_convert_fusion = bf16[320,5120]{1,0:T(8,128)(2,1)} fusion(bf16[5120,128]{1,0:T(8,128)(2,1)} %all-gather.14.cloned.1.call-done, f32[320,512]{1,0:T(8,128)} %get-tuple-element.6, f32[320]{0:T(512)S(1)} %fusion.21, f32[320]{0:T(512)S(1)} %get-tuple-element.5, bf16[512,256]{1,0:T(8,128)(2,1)} %convolution_convert_fusion.1, ...), kind=kOutput, calls=%fused_computation | convolution fusion | flops 463609856 | bytes 5508096 | tf_op jit(solution)/shard_map/dot_general | solution.py:74
  161.8 0.0 reduce-scatter.2.cloned.1.call-update
  161.9 3.5 %convert_element_type.48 = f32[1,320,5120]{2,1,0:T(8,128)} convert(bf16[1,320,5120]{2,1,0:T(8,128)(2,1)S(1)} %copy-done) | non-fusion elementwise | flops 1638400 | bytes 9830400 | tf_op jit(solution)/shard_map/convert_element_type | solution.py:41
  166.0 72.1 %reduce-scatter.2.cloned.1.call-done = bf16[40,5120]{1,0:T(8,128)(2,1)} async-done(((bf16[320,5120]{1,0:T(8,128)(2,1)}), bf16[40,5120]{1,0:T(8,128)(2,1)}) %reduce-scatter.2.cloned.1.call-update) | async-done | bytes 409616 | tf_op jit(solution)/shard_map/reduce_scatter | solution.py:73
  238.1 2.2 fusion.23
  (3 shorter events, 0.0 us)
Async XLA Ops:
  6.5 66.2 %all-gather.8.cloned.1.call-start = ((), (), s32[]{:S(2)}) async-start(), calls=%async_computation.6 | async-start | bytes 1638400 | tf_op jit(solution)/shard_map/all_gather | solution.py:37
  25.8 37.0 %copy-start = (bf16[1,320,5120]{2,1,0:T(8,128)(2,1)S(1)}, bf16[1,320,5120]{2,1,0:T(8,128)(2,1)}, u32[]{:S(2)}) copy-start(bf16[1,320,5120]{2,1,0:T(8,128)(2,1)} %param.12) | copy-start | bytes 9830404
  25.8 47.0 %all-gather.10.cloned.1.call-start = ((), (), s32[]{:S(2)}) async-start(), calls=%async_computation.7 | async-start | bytes 1638400 | tf_op jit(solution)/shard_map/all_gather | solution.py:38
  40.9 78.4 %all-gather.12.cloned.1.call-start = ((), (), s32[]{:S(2)}) async-start(), calls=%async_computation.8 | async-start | bytes 2949120 | tf_op jit(solution)/shard_map/all_gather | solution.py:49
  41.6 95.8 %all-gather.6.cloned.1.call-start = ((), (), s32[]{:S(2)}) async-start(), calls=%async_computation.5 | async-start | bytes 1638400 | tf_op jit(solution)/shard_map/all_gather | solution.py:36
  42.8 28.7 %copy-start.3 = (s32[1,256]{1,0:T(1,128)S(1)}, s32[1,256]{1,0:T(1,128)}, u32[]{:S(2)}) copy-start(s32[1,256]{1,0:T(1,128)} %param.21) | copy-start | bytes 3076
  57.9 12.9 %all-to-all-start.3 = ((bf16[160,8,128]{2,0,1:T(8,128)(2,1)}), bf16[160,8,128]{2,0,1:T(8,128)(2,1)}, u32[]{:S(2)}, u32[]{:S(2)}) async-start(bf16[160,8,128]{2,0,1:T(8,128)(2,1)} %copy_bitcast_fusion), calls=%async_computation.3 | async-start | bytes 655360 | tf_op jit(solution)/shard_map/all_to_all | solution.py:33
  62.0 95.1 %all-gather.14.cloned.1.call-start = ((), (), s32[]{:S(2)}) async-start(), calls=%async_computation.9 | async-start | bytes 1638400 | tf_op jit(solution)/shard_map/all_gather | solution.py:39
  70.9 167.3 %reduce-scatter.2.cloned.1.call-start = ((), (), s32[]{:S(2)}) async-start(), calls=%async_computation.10 | async-start | bytes 3686400 | tf_op jit(solution)/shard_map/reduce_scatter | solution.py:73
  72.7 64.8 %copy-start.2 = (bf16[1,512,128]{2,1,0:T(8,128)(2,1)S(1)}, bf16[1,512,128]{2,1,0:T(8,128)(2,1)}, u32[]{:S(2)}) copy-start(bf16[1,512,128]{2,1,0:T(8,128)(2,1)} %param.18) | copy-start | bytes 393220
  123.7 33.4 %copy-start.1 = (bf16[1,512,128]{2,1,0:T(8,128)(2,1)S(1)}, bf16[1,512,128]{2,1,0:T(8,128)(2,1)}, u32[]{:S(2)}) copy-start(bf16[1,512,128]{2,1,0:T(8,128)(2,1)} %param.19) | copy-start | bytes 393220
Sparse Core Ops, SparseCore 0:
  25.9 16.5 all-gather.7
  44.1 18.1 all-gather.9
  64.5 54.6 all-gather.11
  120.6 16.7 all-gather.5
  138.9 18.1 all-gather.13
  162.0 76.1 reduce-scatter.1
where the time goes:
time: 248 us; the launch traced here: 247 us
  waiting for transfers between devices  155 us (62%)
  blocking collectives  45.1 us (18%)
  between operations  14.9 us (6%)
  other arithmetic  14.8 us (6%)
  matrix products  12.8 us (5%)
  starting transfers between devices  4.28 us (2%)
    reduce_scatter x1, waiting for transfers between devices, on_device(): lax.psum_scatter(lax.dot_general(attended, o_local, (((1,), (1,)), ((), (...  72.1 us
    all_gather x1, waiting for transfers between devices, on_device(): lax.all_gather(text_rows, 'tp', axis=1, tiled=True)  46.5 us
    all_to_all x1, blocking collectives, on_device(): lax.all_to_all(k_half, 'tp', split_axis=1, concat_axis=0, tiled=True)  18.1 us
    all_gather x1, waiting for transfers between devices, on_device(): lax.all_gather(o_block, 'req', axis=0, tiled=True)  14.7 us
    all_gather x1, waiting for transfers between devices, on_device(): lax.all_gather(q_block, 'req', axis=0, tiled=True)  13.8 us
    all_to_all x1, blocking collectives, on_device(): lax.all_to_all(v_half, 'tp', split_axis=1, concat_axis=0, tiled=True)  13.7 us
    all_to_all x1, blocking collectives, on_device(): lax.all_to_all(q_half, 'tp', split_axis=1, concat_axis=0, tiled=True)  13.2 us
    all_to_all x1, waiting for transfers between devices, on_device(): lax.all_to_all(o_half, 'tp', split_axis=1, concat_axis=0, tiled=True)  7.57 us
  transfers between devices with their start and end apart: 7, of which 5 were waited for; matrix products, arithmetic and copies ran while one was open for 8% of the time, Pallas kernels for 0%

commit v1 on v0

--- a/solution.py
+++ b/solution.py
@@ -1,8 +1,11 @@
+import functools
 import math
 
 import jax
 import jax.numpy as jnp
 from jax import lax
+from jax.experimental import pallas as pl
+from jax.experimental.pallas import tpu as pltpu
 from jax.sharding import PartitionSpec as P
 
 
@@ -85,9 +88,358 @@
     return result.astype(jnp.bfloat16)[None]
 
 
+MESH = pl.DeviceIdType.MESH
+BF16 = jnp.bfloat16
+F32 = jnp.float32
+
+
+def flip(index, mask):
+    result = 0
+    for bit in (1, 2, 4):
+        has = (index // bit) % 2
+        result = result + bit * ((1 - has) if mask & bit else has)
+    return result
+
+
+def fused_kernel(
+    hidden,
+    gain,
+    qw,
+    kw,
+    vw,
+    ow,
+    kc,
+    vc,
+    text,
+    tidx,
+    clen,
+    tlen,
+    out,
+    wsend,
+    wall,
+    tall,
+    oall,
+    normed,
+    resid,
+    att,
+    ftot,
+    fsend,
+    frecv,
+    w_ss,
+    w_rs,
+    x_ss,
+    t_ss,
+    t_rs,
+    o_ss,
+    o_rs,
+    a_ss,
+    a_rs,
+    f_ss,
+    f_rs,
+):
+    slots, width = hidden.shape
+    block = qw.shape[0]
+    text_total, hd = kc.shape
+    r = lax.axis_index("req")
+    t = lax.axis_index("tp")
+    z, y = t // 2, t % 2
+    r1 = r + 1 - 2 * (r % 2)
+    r2 = (r + 2) % 4
+    r3 = (r1 + 2) % 4
+    me = r * 8 + t
+
+    def send(src, dst, ss, rs, **dev):
+        return pltpu.make_async_remote_copy(
+            src_ref=src, dst_ref=dst, send_sem=ss, recv_sem=rs, device_id=dev, device_id_type=MESH
+        )
+
+    barrier = pltpu.get_barrier_semaphore()
+    for i in range(1, 8):
+        pl.semaphore_signal(barrier, inc=1, device_id={"tp": flip(t, i)}, device_id_type=MESH)
+    for peer in (r1, r2):
+        pl.semaphore_signal(barrier, inc=1, device_id={"req": peer}, device_id_type=MESH)
+
+    tall[t] = text[...]
+    for h in range(8):
+        cols = slice(h * hd, (h + 1) * hd)
+        wsend[h] = jnp.concatenate(
+            [qw[:, cols].astype(BF16), kw[:, cols].astype(BF16), vw[:, cols].astype(BF16)], axis=1
+        )
+    wall[me] = wsend[t]
+    oall[r] = ow[...].astype(BF16)
+    pl.semaphore_wait(barrier, 9)
+
+    def text_copy(shard, way, sem):
+        slot = 2 * shard + y
+        if way == 0:
+            target = 2 * z + 1 - y
+        else:
+            target = 2 * (z + way) + y
+        return send(tall.at[slot], tall.at[slot], t_ss.at[sem], t_rs.at[slot], tp=target)
+
+    def text_step(d, wait_send=False):
+        for side in (1, -1):
+            if d == 0 and side == -1:
+                continue
+            shard = z - side * d
+            inside = (shard >= 0) & (shard <= 3)
+            base = 3 * (2 * d + (side < 0))
+
+            @pl.when(inside)
+            def _():
+                if d > 0 and not wait_send:
+                    text_copy(shard, 0, base).wait_recv()
+                across = text_copy(shard, 0, base)
+                if wait_send:
+                    across.wait_send()
+                else:
+                    across.start()
+                for way in (1, -1):
+                    if d > 0 and way != side:
+                        continue
+                    onward = text_copy(shard, way, base + (1 if way == 1 else 2))
+
+                    @pl.when((z + way >= 0) & (z + way <= 3))
+                    def _():
+                        if wait_send:
+                            onward.wait_send()
+                        else:
+                            onward.start()
+
+    text_step(0)
+
+    o_copies = [
+        send(oall.at[r], oall.at[r], o_ss.at[0], o_rs.at[r], req=r1),
+        send(oall.at[r], oall.at[r], o_ss.at[1], o_rs.at[r], req=r2),
+        send(oall.at[r2], oall.at[r2], o_ss.at[2], o_rs.at[r2], req=r1),
+    ]
+    w_copies = [
+        send(wsend.at[flip(t, i)], wall.at[me], w_ss.at[i], w_rs.at[me], tp=flip(t, i))
+        for i in range(1, 8)
+    ]
+
+    def onward(i, which):
+        if which == 2:
+            slot, target = r2 * 8 + flip(t, i), r1
+        else:
+            slot, target = r * 8 + flip(t, i), (r1 if which == 0 else r2)
+        return send(wall.at[slot], wall.at[slot], x_ss.at[8 * which + i], w_rs.at[slot], req=target)
+
+    def w_arrived(owner, i):
+        slot = owner * 8 + flip(t, i)
+        send(wall.at[slot], wall.at[slot], w_ss.at[0], w_rs.at[slot], req=r1).wait_recv()
+
+    def o_arrived(owner):
+        send(oall.at[owner], oall.at[owner], o_ss.at[0], o_rs.at[owner], req=r1).wait_recv()
+
+    for copy in w_copies:
+        copy.start()
+    onward(0, 1).start()
+    onward(0, 0).start()
+    o_copies[1].start()
+    o_copies[0].start()
+
+    def norm_rows(c, carry):
+        rows = pl.ds(pl.multiple_of(c * 16, 16), 16)
+        x = hidden[rows, :].astype(F32)
+        mean = jnp.mean(x, axis=-1, keepdims=True)
+        centered = x - mean
+        var = jnp.mean(centered * centered, axis=-1, keepdims=True)
+        normed[rows, :] = (centered * lax.rsqrt(var + 1e-06) * gain[...]).astype(BF16)
+        return carry
+
+    lax.fori_loop(0, slots // 16, norm_rows, 0)
+
+    text_step(1)
+    for i in (1, 2, 3):
+        w_arrived(r, i)
+        onward(i, 1).start()
+        onward(i, 0).start()
+    text_step(2)
+    for i in (4, 5, 6, 7):
+        w_arrived(r, i)
+        onward(i, 1).start()
+        onward(i, 0).start()
+    text_step(3)
+
+    span = 8 * block
+    picked = (
+        lax.broadcasted_iota(jnp.int32, (span, block), 0)
+        == lax.broadcasted_iota(jnp.int32, (span, block), 1) + t * block
+    )
+    pick = jnp.where(picked, 1.0, 0.0).astype(BF16)
+    resid[...] = jnp.concatenate(
+        [
+            jnp.dot(hidden[:, g * span : (g + 1) * span], pick, preferred_element_type=F32)
+            for g in range(4)
+        ],
+        axis=1,
+    )
+
+    for i in range(8):
+        w_arrived(r2, i)
+        onward(i, 2).start()
+    o_arrived(r2)
+    o_copies[2].start()
+    for i in range(8):
+        w_arrived(r1, i)
+    for i in range(8):
+        w_arrived(r3, i)
+    for shard in range(4):
+        slot = 2 * shard + 1 - y
+        send(tall.at[slot], tall.at[slot], t_ss.at[0], t_rs.at[slot], tp=flip(t, 1)).wait_recv()
+
+    query = jnp.zeros((slots, hd), F32)
+    fresh = jnp.zeros((8 * text.shape[0], 2 * hd), F32)
+    for g in range(4):
+        cols = slice(g * span, (g + 1) * span)
+        part = slice(8 * g, 8 * g + 8)
+        query += jnp.dot(
+            normed[:, cols],
+            wall[part, :, 0:hd].reshape(span, hd),
+            preferred_element_type=F32,
+        )
+        fresh += jnp.dot(
+            tall[:, :, cols].reshape(8 * text.shape[0], span),
+            wall[part, :, hd : 3 * hd].reshape(span, 2 * hd),
+            preferred_element_type=F32,
+        )
+    query = query.astype(BF16)
+    fresh = fresh.astype(BF16)
+
+    recomp = tidx.shape[1]
+    row = lax.broadcasted_iota(jnp.int32, (text_total, recomp), 0)
+    selector = jnp.where(tidx[...] == row, 1.0, 0.0)
+    covered = jnp.sum(selector, axis=1, keepdims=True) > 0.5
+    placed = jnp.dot(selector.astype(BF16), fresh, preferred_element_type=F32)
+    keys = jnp.where(covered, placed[:, :hd], kc[...].astype(F32)).astype(BF16)
+    values = jnp.where(covered, placed[:, hd:], vc[...].astype(F32)).astype(BF16)
+    score = lax.dot_general(query, keys, (((1,), (1,)), ((), ())), preferred_element_type=F32)
+    score = score * (1.0 / math.sqrt(hd))
+    column = lax.broadcasted_iota(jnp.int32, score.shape, 1)
+    score = jnp.where(column < tlen[0], score, -1e30)
+    top = jnp.max(score, axis=-1, keepdims=True)
+    expo = jnp.exp(score - top)
+    weights = (expo / jnp.sum(expo, axis=-1, keepdims=True)).astype(BF16)
+    att[t] = jnp.dot(weights, values, preferred_element_type=F32).astype(BF16)
+
+    a_copies = [
+        send(att.at[t], att.at[t], a_ss.at[i], a_rs.at[t], tp=flip(t, i)) for i in range(1, 8)
+    ]
+    for copy in a_copies:
+        copy.start()
+    o_arrived(r1)
+    o_arrived(r3)
+    for i in range(1, 8):
+        slot = flip(t, i)
+        send(att.at[slot], att.at[slot], a_ss.at[0], a_rs.at[slot], tp=slot).wait_recv()
+
+    step = 80
+    for c in range(slots // step):
+        total = jnp.zeros((step, 4 * block), F32)
+        for h in range(8):
+            term = lax.dot_general(
+                att[h, c * step : (c + 1) * step, :],
+                oall[:, :, h * hd : (h + 1) * hd].reshape(4 * block, hd),
+                (((1,), (1,)), ((), ())),
+                preferred_element_type=F32,
+            )
+            total += term.astype(BF16).astype(F32)
+        position = lax.broadcasted_iota(jnp.int32, total.shape, 0) + c * step
+        rows = slice(c * step, (c + 1) * step)
+        ftot[rows, :] = resid[rows, :] + jnp.where(position < clen[0], total, 0.0)
+    local = slots // 8
+    padded = fsend.shape[1]
+    ftot[slots : slots + padded - local, :] = jnp.zeros((padded - local, 4 * block), F32)
+    for j in range(8):
+        fsend[j] = ftot[j * local : j * local + padded, :].astype(BF16)
+    f_copies = [
+        send(fsend.at[flip(t, i)], frecv.at[t], f_ss.at[i], f_rs.at[t], tp=flip(t, i))
+        for i in range(1, 8)
+    ]
+    for copy in f_copies:
+        copy.start()
+    frecv[t] = fsend[t]
+    for i in range(1, 8):
+        slot = flip(t, i)
+        send(frecv.at[slot], frecv.at[slot], f_ss.at[0], f_rs.at[slot], tp=slot).wait_recv()
+    for g in range(4):
+        pieces = [
+            frecv[j].astype(F32)[:local, g * block : (g + 1) * block] for j in range(8)
+        ]
+        out[:, g * span : (g + 1) * span] = jnp.concatenate(pieces, axis=1).astype(BF16)
+
+    for d in range(4):
+        text_step(d, wait_send=True)
+    for copy in w_copies + o_copies + a_copies + f_copies:
+        copy.wait_send()
+    for which in range(3):
+        for i in range(8):
+            onward(i, which).wait_send()
+
+
+def fused(hidden, gain, qw, kw, vw, ow, kc, vc, text, tidx, clen, tlen):
+    _, slots, width = hidden.shape
+    block, inner = qw.shape
+    _, text_total, hd = kc.shape
+    local = slots // 8
+    padded = -(-local // 16) * 16
+    vmem = pl.BlockSpec(memory_space=pltpu.VMEM)
+    smem = pl.BlockSpec(memory_space=pltpu.SMEM)
+    dma = pltpu.SemaphoreType.DMA
+    result = pl.pallas_call(
+        fused_kernel,
+        out_shape=jax.ShapeDtypeStruct((local, width), BF16),
+        in_specs=[vmem] * 10 + [smem] * 2,
+        out_specs=vmem,
+        scratch_shapes=[
+            pltpu.VMEM((8, block, 3 * hd), BF16),
+            pltpu.VMEM((32, block, 3 * hd), BF16),
+            pltpu.VMEM((8, text.shape[1], width), BF16),
+            pltpu.VMEM((4, block, inner), BF16),
+            pltpu.VMEM((slots, width), BF16),
+            pltpu.VMEM((slots, 4 * block), F32),
+            pltpu.VMEM((8, slots, hd), BF16),
+            pltpu.VMEM((slots + padded - local, 4 * block), F32),
+            pltpu.VMEM((8, padded, 4 * block), BF16),
+            pltpu.VMEM((8, padded, 4 * block), BF16),
+            dma((8,)),
+            dma((32,)),
+            dma((24,)),
+            dma((24,)),
+            dma((8,)),
+            dma((3,)),
+            dma((4,)),
+            dma((8,)),
+            dma((8,)),
+            dma((8,)),
+            dma((8,)),
+        ],
+        compiler_params=pltpu.CompilerParams(
+            collective_id=0, has_side_effects=True, vmem_limit_bytes=56 * 1024 * 1024
+        ),
+        cost_estimate=pl.CostEstimate(
+            flops=3 * 10**9, bytes_accessed=10**7, transcendentals=slots * text_total
+        ),
+    )(
+        hidden[0], gain[None], qw, kw, vw, ow, kc[0], vc[0], text[0], tidx, clen, tlen
+    )
+    return result[None]
+
+
 def solution(mesh):
+    def run(*args):
+        hidden, qw, text = args[0], args[2], args[8]
+        fits = (
+            (mesh.shape["req"], mesh.shape["tp"]) == (4, 8)
+            and qw.shape[0] % 16 == 0
+            and text.shape[1] % 16 == 0
+            and hidden.shape[1] % 80 == 0
+        )
+        return (fused if fits else on_device)(*args)
+
     return jax.shard_map(
-        on_device,
+        run,
         mesh=mesh,
         in_specs=(
             P("req", None, None),

time: 248 us -> 94.9 us (0.38)
  waiting for transfers between devices: 155 us -> 0 us
  Pallas kernels: 0 us -> 91.3 us
  blocking collectives: 45.1 us -> 0 us
  other arithmetic: 14.8 us -> 0 us
  between operations: 14.9 us -> 1.3 us
  matrix products: 12.8 us -> 0 us
  starting transfers between devices: 4.28 us -> 0 us
    pallas_call x0 -> x1, Pallas kernels: none -> 91.3 us  [fused(): pl.pallas_call(fused_kernel, out_shape=jax.ShapeDtypeStruct((local, width...]
    all_gather x5 -> x0, waiting for transfers between devices: 74.9 us -> none  [the longest x1 46.5 us: on_device(): lax.all_gather(text_rows, 'tp', axis=1, tiled=True)]
    reduce_scatter x1 -> x0, waiting for transfers between devices: 72.1 us -> none  [on_device(): lax.psum_scatter(lax.dot_general(attended, o_local, (((1,), (1,)), ((), (...]
    all_to_all x3 -> x0, blocking collectives: 45.1 us -> none  [the longest x1 18.1 us: on_device(): lax.all_to_all(k_half, 'tp', split_axis=1, concat_axis=0, tiled=True)]
    dot_general x3 -> x0, matrix products: 12.8 us -> none  [the longest x1 4.75 us: on_device(): lax.dot_general(attended, o_local, (((1,), (1,)), ((), ())), preferred_el...]
    all_to_all x1 -> x0, waiting for transfers between devices: 7.57 us -> none  [on_device(): lax.all_to_all(o_half, 'tp', split_axis=1, concat_axis=0, tiled=True)]
    all_to_all x4 -> x0, other arithmetic: 5.42 us -> none  [the longest x1 1.87 us: on_device(): lax.all_to_all(o_half, 'tp', split_axis=1, concat_axis=0, tiled=True)]
    all_to_all x1 -> x0, starting transfers between devices: 4.08 us -> none  [on_device(): lax.all_to_all(o_half, 'tp', split_axis=1, concat_axis=0, tiled=True)]
  transfers between devices with their start and end apart: 7 -> 0, of which waited for: 5 -> 0; matrix products, arithmetic and copies ran while one was open for 8% -> 0% of each run, Pallas kernels for 0% -> 0%
where the time goes in v1:
time: 94.9 us; the launch traced here: 94.4 us
  Pallas kernels  91.3 us (96%)
  local copies, waits for them, and re-layouts  1.78 us (2%)
  between operations  1.3 us (1%)
    pallas_call x1, Pallas kernels, fused(): pl.pallas_call(fused_kernel, out_shape=jax.ShapeDtypeStruct((local, width...  91.3 us

profile of v1, /device:TPU:0, one launch (start us, length us, event | category | flops | bytes accessed | tf_op | source)
XLA Modules:
  0.0 94.4 jit_solution(12066288689923576784)
XLA Ops:
  1.3 91.3 %shard_map.118 = bf16[40,5120]{1,0:T(8,128)(2,1)} custom-call(bf16[320,5120]{1,0:T(8,128)(2,1)} %bitcast.7, f32[1,5120]{1,0:T(1,128)} %bitcast.11, f32[160,1024]{1,0:T(8,128)} %qw.1, f32[160,1024]{1,0:T(8,128)} %kw.1, f32[160,1024]{1,0:T(8,128)} %vw.1, f32[160,1024]{1,0:T(8,128)} %ow.1, bf16[512,128]{1,0:T(8,128)(2,1)} %bitcast.9, ...), custom_call_target="tpu_custom_call" | custom-call | flops 3000000000 | bytes 10000000 | tf_op jit(solution)/shard_map/pallas_call | solution.py:390
  92.6 1.8 %copy.16 = bf16[1,40,5120]{2,1,0:T(8,128)(2,1)} copy(bf16[1,40,5120]{2,1,0:T(8,128)(2,1)} %bitcast.6) | data formatting | bytes 819200

commit v2 on v1

--- a/solution.py
+++ b/solution.py
@@ -102,7 +102,7 @@
 
 
 def fused_kernel(
-    hidden,
+    hidden_hbm,
     gain,
     qw,
     kw,
@@ -115,6 +115,10 @@
     clen,
     tlen,
     out,
+    hidden,
+    freshbuf,
+    selector,
+    covering,
     wsend,
     wall,
     tall,
@@ -136,6 +140,7 @@
     a_rs,
     f_ss,
     f_rs,
+    h_sem,
 ):
     slots, width = hidden.shape
     block = qw.shape[0]
@@ -159,7 +164,9 @@
     for peer in (r1, r2):
         pl.semaphore_signal(barrier, inc=1, device_id={"req": peer}, device_id_type=MESH)
 
-    tall[t] = text[...]
+    hidden_copy = pltpu.make_async_copy(hidden_hbm, hidden, h_sem)
+    hidden_copy.start()
+    tall[y, z] = text[...]
     for h in range(8):
         cols = slice(h * hd, (h + 1) * hd)
         wsend[h] = jnp.concatenate(
@@ -169,35 +176,31 @@
     oall[r] = ow[...].astype(BF16)
     pl.semaphore_wait(barrier, 9)
 
-    def text_copy(shard, way, sem):
-        slot = 2 * shard + y
-        if way == 0:
-            target = 2 * z + 1 - y
-        else:
-            target = 2 * (z + way) + y
-        return send(tall.at[slot], tall.at[slot], t_ss.at[sem], t_rs.at[slot], tp=target)
-
-    def text_step(d, wait_send=False):
+    def chain_copy(ref, ss, rs, part, shard, way, sem):
+        target = 2 * z + 1 - y if way == 0 else 2 * (z + way) + y
+        piece = ref(y, shard, part)
+        slot = rs.shape[0] // 8 * (4 * y + shard) + part
+        return send(piece, piece, ss.at[sem], rs.at[slot], tp=target)
+
+    def chain_step(ref, ss, rs, part, d, wait_send=False, then=None):
+        parts = rs.shape[0] // 8
         for side in (1, -1):
             if d == 0 and side == -1:
                 continue
             shard = z - side * d
-            inside = (shard >= 0) & (shard <= 3)
-            base = 3 * (2 * d + (side < 0))
-
-            @pl.when(inside)
+            base = 3 * (parts * (2 * d + (side < 0)) + part)
+
+            @pl.when((shard >= 0) & (shard <= 3))
             def _():
+                across = chain_copy(ref, ss, rs, part, shard, 0, base)
                 if d > 0 and not wait_send:
-                    text_copy(shard, 0, base).wait_recv()
-                across = text_copy(shard, 0, base)
-                if wait_send:
-                    across.wait_send()
-                else:
-                    across.start()
+                    across.wait_recv()
                 for way in (1, -1):
                     if d > 0 and way != side:
                         continue
-                    onward = text_copy(shard, way, base + (1 if way == 1 else 2))
+                    onward = chain_copy(
+                        ref, ss, rs, part, shard, way, base + (1 if way == 1 else 2)
+                    )
 
                     @pl.when((z + way >= 0) & (z + way <= 3))
                     def _():
@@ -205,6 +208,28 @@
                             onward.wait_send()
                         else:
                             onward.start()
+
+                if wait_send:
+                    across.wait_send()
+                else:
+                    across.start()
+                if then is not None:
+                    then(y, shard)
+
+    def crossed(ref, ss, rs, part, shard):
+        piece = ref(1 - y, shard, part)
+        slot = rs.shape[0] // 8 * (4 * (1 - y) + shard) + part
+        send(piece, piece, ss.at[0], rs.at[slot], tp=flip(t, 1)).wait_recv()
+
+    def text_ref(column, shard, part):
+        return tall.at[column, shard, part]
+
+    def att_ref(column, shard, part):
+        return att.at[2 * shard + column]
+
+    def text_step(d, wait_send=False):
+        for part in range(2):
+            chain_step(text_ref, t_ss, t_rs, part, d, wait_send)
 
     text_step(0)
 
@@ -248,6 +273,7 @@
         normed[rows, :] = (centered * lax.rsqrt(var + 1e-06) * gain[...]).astype(BF16)
         return carry
 
+    hidden_copy.wait()
     lax.fori_loop(0, slots // 16, norm_rows, 0)
 
     text_step(1)
@@ -275,43 +301,52 @@
         ],
         axis=1,
     )
+    recomp = tidx.shape[1]
+    row = lax.broadcasted_iota(jnp.int32, (text_total, recomp), 0)
+    chosen = jnp.where(tidx[...] == row, 1.0, 0.0)
+    selector[...] = chosen.astype(BF16)
+    covering[...] = jnp.broadcast_to(jnp.sum(chosen, axis=1, keepdims=True), covering.shape)
+
+    def query_part(g):
+        return jnp.dot(
+            normed[:, pl.ds(pl.multiple_of(g * span, span), span)],
+            wall[pl.ds(8 * g, 8), :, 0:hd].reshape(span, hd),
+            preferred_element_type=F32,
+        )
 
     for i in range(8):
         w_arrived(r2, i)
         onward(i, 2).start()
     o_arrived(r2)
     o_copies[2].start()
+    query = query_part(r) + query_part(r2)
     for i in range(8):
         w_arrived(r1, i)
+    query += query_part(r1)
     for i in range(8):
         w_arrived(r3, i)
+    query += query_part(r3)
+    query = query.astype(BF16)
+
+    shard_rows = text.shape[0] * text.shape[1]
+
+    def fresh_rows(column):
+        lines = tall[column].reshape(4 * shard_rows, 4 * span)
+        part = jnp.dot(
+            lines, wall[:, :, hd : 3 * hd].reshape(4 * span, 2 * hd), preferred_element_type=F32
+        ).astype(BF16)
+        for shard in range(4):
+            freshbuf[2 * shard + column] = part[shard * shard_rows : (shard + 1) * shard_rows]
+
+    fresh_rows(y)
     for shard in range(4):
-        slot = 2 * shard + 1 - y
-        send(tall.at[slot], tall.at[slot], t_ss.at[0], t_rs.at[slot], tp=flip(t, 1)).wait_recv()
-
-    query = jnp.zeros((slots, hd), F32)
-    fresh = jnp.zeros((8 * text.shape[0], 2 * hd), F32)
-    for g in range(4):
-        cols = slice(g * span, (g + 1) * span)
-        part = slice(8 * g, 8 * g + 8)
-        query += jnp.dot(
-            normed[:, cols],
-            wall[part, :, 0:hd].reshape(span, hd),
-            preferred_element_type=F32,
-        )
-        fresh += jnp.dot(
-            tall[:, :, cols].reshape(8 * text.shape[0], span),
-            wall[part, :, hd : 3 * hd].reshape(span, 2 * hd),
-            preferred_element_type=F32,
-        )
-    query = query.astype(BF16)
-    fresh = fresh.astype(BF16)
-
-    recomp = tidx.shape[1]
-    row = lax.broadcasted_iota(jnp.int32, (text_total, recomp), 0)
-    selector = jnp.where(tidx[...] == row, 1.0, 0.0)
-    covered = jnp.sum(selector, axis=1, keepdims=True) > 0.5
-    placed = jnp.dot(selector.astype(BF16), fresh, preferred_element_type=F32)
+        for part in range(2):
+            crossed(text_ref, t_ss, t_rs, part, shard)
+    fresh_rows(1 - y)
+    fresh = freshbuf[...].reshape(recomp, 2 * hd)
+
+    covered = covering[...] > 0.5
+    placed = jnp.dot(selector[...], fresh, preferred_element_type=F32)
     keys = jnp.where(covered, placed[:, :hd], kc[...].astype(F32)).astype(BF16)
     values = jnp.where(covered, placed[:, hd:], vc[...].astype(F32)).astype(BF16)
     score = lax.dot_general(query, keys, (((1,), (1,)), ((), ())), preferred_element_type=F32)
@@ -323,55 +358,85 @@
     weights = (expo / jnp.sum(expo, axis=-1, keepdims=True)).astype(BF16)
     att[t] = jnp.dot(weights, values, preferred_element_type=F32).astype(BF16)
 
-    a_copies = [
-        send(att.at[t], att.at[t], a_ss.at[i], a_rs.at[t], tp=flip(t, i)) for i in range(1, 8)
-    ]
-    for copy in a_copies:
-        copy.start()
+    chain_step(att_ref, a_ss, a_rs, 0, 0)
     o_arrived(r1)
     o_arrived(r3)
-    for i in range(1, 8):
-        slot = flip(t, i)
-        send(att.at[slot], att.at[slot], a_ss.at[0], a_rs.at[slot], tp=slot).wait_recv()
-
-    step = 80
-    for c in range(slots // step):
-        total = jnp.zeros((step, 4 * block), F32)
-        for h in range(8):
-            term = lax.dot_general(
-                att[h, c * step : (c + 1) * step, :],
-                oall[:, :, h * hd : (h + 1) * hd].reshape(4 * block, hd),
-                (((1,), (1,)), ((), ())),
-                preferred_element_type=F32,
-            )
-            total += term.astype(BF16).astype(F32)
+    local = slots // 8
+    step = 2 * local
+    features = 4 * block
+
+    def head_rows(slot, c):
+        rows = pl.ds(pl.multiple_of(c * step, 16), step)
+        head = pl.ds(pl.multiple_of(slot * hd, hd), hd)
+        term = lax.dot_general(
+            att[slot, rows, :],
+            oall[:, :, head].reshape(features, hd),
+            (((1,), (1,)), ((), ())),
+            preferred_element_type=F32,
+        )
+        return rows, term.astype(BF16).astype(F32)
+
+    def add_head(column, shard):
+        def body(c, carry):
+            rows, term = head_rows(2 * shard + column, c)
+            ftot[rows, :] += term
+            return carry
+
+        lax.fori_loop(0, 4, body, 0)
+
+    ftot[...] = jnp.zeros_like(ftot)
+    add_head(y, z)
+    for d in (1, 2, 3):
+        chain_step(att_ref, a_ss, a_rs, 0, d, then=add_head)
+
+    def z_flip(mask):
+        return flip(t, 2 * mask) // 2
+
+    for m in (0, 1, 3, 2):
+        crossed(att_ref, a_ss, a_rs, 0, z_flip(m))
+        if m != 2:
+            add_head(1 - y, z_flip(m))
+
+    tiles = features // 128
+    padded = fsend.shape[1]
+    f_copies = []
+    for m in (3, 2, 1, 0):
+        c = z_flip(m)
+        rows, term = head_rows(2 * z_flip(2) + 1 - y, c)
+        total = ftot[rows, :] + term
         position = lax.broadcasted_iota(jnp.int32, total.shape, 0) + c * step
-        rows = slice(c * step, (c + 1) * step)
-        ftot[rows, :] = resid[rows, :] + jnp.where(position < clen[0], total, 0.0)
-    local = slots // 8
-    padded = fsend.shape[1]
-    ftot[slots : slots + padded - local, :] = jnp.zeros((padded - local, 4 * block), F32)
-    for j in range(8):
-        fsend[j] = ftot[j * local : j * local + padded, :].astype(BF16)
-    f_copies = [
-        send(fsend.at[flip(t, i)], frecv.at[t], f_ss.at[i], f_rs.at[t], tp=flip(t, i))
-        for i in range(1, 8)
-    ]
-    for copy in f_copies:
-        copy.start()
+        total = resid[rows, :] + jnp.where(position < clen[0], total, 0.0)
+        for half in range(2):
+            own = total[half * local : (half + 1) * local]
+            pieces = [own[:, k * 128 : (k + 1) * 128] for k in range(tiles)]
+            if padded > tiles * local:
+                pieces.append(jnp.zeros((padded - tiles * local, 128), F32))
+            fsend[2 * c + half] = jnp.concatenate(pieces, axis=0).astype(BF16)
+        for i in (2 * m, 2 * m + 1):
+            if i > 0:
+                copy = send(
+                    fsend.at[flip(t, i)], frecv.at[t], f_ss.at[i], f_rs.at[t], tp=flip(t, i)
+                )
+                copy.start()
+                f_copies.append(copy)
     frecv[t] = fsend[t]
     for i in range(1, 8):
         slot = flip(t, i)
         send(frecv.at[slot], frecv.at[slot], f_ss.at[0], f_rs.at[slot], tp=slot).wait_recv()
+    lines = []
+    for j in range(8):
+        got = frecv[j].astype(F32)
+        lines.append(
+            jnp.concatenate([got[k * local : (k + 1) * local] for k in range(tiles)], axis=1)
+        )
     for g in range(4):
-        pieces = [
-            frecv[j].astype(F32)[:local, g * block : (g + 1) * block] for j in range(8)
-        ]
+        pieces = [line[:, g * block : (g + 1) * block] for line in lines]
         out[:, g * span : (g + 1) * span] = jnp.concatenate(pieces, axis=1).astype(BF16)
 
     for d in range(4):
         text_step(d, wait_send=True)
-    for copy in w_copies + o_copies + a_copies + f_copies:
+        chain_step(att_ref, a_ss, a_rs, 0, d, wait_send=True)
+    for copy in w_copies + o_copies + f_copies:
         copy.wait_send()
     for which in range(3):
         for i in range(8):
@@ -383,37 +448,44 @@
     block, inner = qw.shape
     _, text_total, hd = kc.shape
     local = slots // 8
-    padded = -(-local // 16) * 16
+    tiles = 4 * block // 128
+    padded = -(-tiles * local // 16) * 16
+    pieces = text[0].reshape(2, text.shape[1] // 2, width)
     vmem = pl.BlockSpec(memory_space=pltpu.VMEM)
     smem = pl.BlockSpec(memory_space=pltpu.SMEM)
     dma = pltpu.SemaphoreType.DMA
     result = pl.pallas_call(
         fused_kernel,
         out_shape=jax.ShapeDtypeStruct((local, width), BF16),
-        in_specs=[vmem] * 10 + [smem] * 2,
+        in_specs=[pl.BlockSpec(memory_space=pltpu.HBM)] + [vmem] * 9 + [smem] * 2,
         out_specs=vmem,
         scratch_shapes=[
+            pltpu.VMEM((slots, width), BF16),
+            pltpu.VMEM((8, text.shape[1], 2 * hd), BF16),
+            pltpu.VMEM((text_total, tidx.shape[1]), BF16),
+            pltpu.VMEM((text_total, hd), F32),
             pltpu.VMEM((8, block, 3 * hd), BF16),
             pltpu.VMEM((32, block, 3 * hd), BF16),
-            pltpu.VMEM((8, text.shape[1], width), BF16),
+            pltpu.VMEM((2, 4, *pieces.shape), BF16),
             pltpu.VMEM((4, block, inner), BF16),
             pltpu.VMEM((slots, width), BF16),
             pltpu.VMEM((slots, 4 * block), F32),
             pltpu.VMEM((8, slots, hd), BF16),
-            pltpu.VMEM((slots + padded - local, 4 * block), F32),
-            pltpu.VMEM((8, padded, 4 * block), BF16),
-            pltpu.VMEM((8, padded, 4 * block), BF16),
+            pltpu.VMEM((slots, 4 * block), F32),
+            pltpu.VMEM((8, padded, 128), BF16),
+            pltpu.VMEM((8, padded, 128), BF16),
             dma((8,)),
             dma((32,)),
             dma((24,)),
-            dma((24,)),
-            dma((8,)),
+            dma((48,)),
+            dma((16,)),
             dma((3,)),
             dma((4,)),
+            dma((24,)),
             dma((8,)),
             dma((8,)),
             dma((8,)),
-            dma((8,)),
+            dma(()),
         ],
         compiler_params=pltpu.CompilerParams(
             collective_id=0, has_side_effects=True, vmem_limit_bytes=56 * 1024 * 1024
@@ -422,7 +494,7 @@
             flops=3 * 10**9, bytes_accessed=10**7, transcendentals=slots * text_total
         ),
     )(
-        hidden[0], gain[None], qw, kw, vw, ow, kc[0], vc[0], text[0], tidx, clen, tlen
+        hidden[0], gain[None], qw, kw, vw, ow, kc[0], vc[0], pieces, tidx, clen, tlen
     )
     return result[None]
 
@@ -433,7 +505,8 @@
         fits = (
             (mesh.shape["req"], mesh.shape["tp"]) == (4, 8)
             and qw.shape[0] % 16 == 0
-            and text.shape[1] % 16 == 0
+            and text.shape[1] % 32 == 0
+            and qw.shape[0] % 32 == 0
             and hidden.shape[1] % 80 == 0
         )
         return (fused if fits else on_device)(*args)

time: 94.9 us -> 88.9 us (0.937)
  Pallas kernels: 91.3 us -> 85 us
    pallas_call x1, Pallas kernels: 91.3 us -> 85 us  [fused(): pl.pallas_call(fused_kernel, out_shape=jax.ShapeDtypeStruct((local, width...]
where the time goes in v2:
time: 88.9 us; the launch traced here: 88.1 us
  Pallas kernels  85 us (96%)
  local copies, waits for them, and re-layouts  1.78 us (2%)
  between operations  1.3 us (1%)
    pallas_call x1, Pallas kernels, fused(): pl.pallas_call(fused_kernel, out_shape=jax.ShapeDtypeStruct((local, width...  85 us
    unnamed x1, local copies, waits for them, and re-layouts  1.78 us

profile of v2, /device:TPU:0, one launch (start us, length us, event | category | flops | bytes accessed | tf_op | source)
XLA Modules:
  0.0 88.1 jit_solution(14670007899283758635)
XLA Ops:
  1.3 85.0 %shard_map.118 = bf16[40,5120]{1,0:T(8,128)(2,1)} custom-call(bf16[320,5120]{1,0:T(8,128)(2,1)} %bitcast.7, f32[1,5120]{1,0:T(1,128)} %bitcast.11, f32[160,1024]{1,0:T(8,128)} %qw.1, f32[160,1024]{1,0:T(8,128)} %kw.1, f32[160,1024]{1,0:T(8,128)} %vw.1, f32[160,1024]{1,0:T(8,128)} %ow.1, bf16[512,128]{1,0:T(8,128)(2,1)} %bitcast.9, ...), custom_call_target="tpu_custom_call" | custom-call | flops 3000000000 | bytes 10000000 | tf_op jit(solution)/shard_map/pallas_call | solution.py:457
  86.3 1.8 %copy.16 = bf16[1,40,5120]{2,1,0:T(8,128)(2,1)} copy(bf16[1,40,5120]{2,1,0:T(8,128)(2,1)} %bitcast.6) | data formatting | bytes 819200

commit v3 on v2

--- a/solution.py
+++ b/solution.py
@@ -257,7 +257,7 @@
     def o_arrived(owner):
         send(oall.at[owner], oall.at[owner], o_ss.at[0], o_rs.at[owner], req=r1).wait_recv()
 
-    for copy in w_copies:
+    for copy in w_copies[:3]:
         copy.start()
     onward(0, 1).start()
     onward(0, 0).start()
@@ -273,10 +273,10 @@
         normed[rows, :] = (centered * lax.rsqrt(var + 1e-06) * gain[...]).astype(BF16)
         return carry
 
-    hidden_copy.wait()
-    lax.fori_loop(0, slots // 16, norm_rows, 0)
 
     text_step(1)
+    for copy in w_copies[3:]:
+        copy.start()
     for i in (1, 2, 3):
         w_arrived(r, i)
         onward(i, 1).start()
@@ -288,6 +288,8 @@
         onward(i, 0).start()
     text_step(3)
 
+    hidden_copy.wait()
+    lax.fori_loop(0, slots // 16, norm_rows, 0)
     span = 8 * block
     picked = (
         lax.broadcasted_iota(jnp.int32, (span, block), 0)

time: 88.9 us -> 84 us (0.945)
  Pallas kernels: 85 us -> 80.7 us
    pallas_call x1, Pallas kernels: 85 us -> 80.7 us  [fused(): pl.pallas_call(fused_kernel, out_shape=jax.ShapeDtypeStruct((local, width...]
where the time goes in v3:
time: 84 us; the launch traced here: 83.8 us
  Pallas kernels  80.7 us (96%)
  local copies, waits for them, and re-layouts  1.78 us (2%)
  between operations  1.3 us (2%)
    pallas_call x1, Pallas kernels, fused(): pl.pallas_call(fused_kernel, out_shape=jax.ShapeDtypeStruct((local, width...  80.7 us
    unnamed x1, local copies, waits for them, and re-layouts  1.78 us

profile of v3, /device:TPU:0, one launch (start us, length us, event | category | flops | bytes accessed | tf_op | source)
XLA Modules:
  0.0 83.8 jit_solution(291278745605924909)
XLA Ops:
  1.3 80.7 %shard_map.118 = bf16[40,5120]{1,0:T(8,128)(2,1)} custom-call(bf16[320,5120]{1,0:T(8,128)(2,1)} %bitcast.7, f32[1,5120]{1,0:T(1,128)} %bitcast.11, f32[160,1024]{1,0:T(8,128)} %qw.1, f32[160,1024]{1,0:T(8,128)} %kw.1, f32[160,1024]{1,0:T(8,128)} %vw.1, f32[160,1024]{1,0:T(8,128)} %ow.1, bf16[512,128]{1,0:T(8,128)(2,1)} %bitcast.9, ...), custom_call_target="tpu_custom_call" | custom-call | flops 3000000000 | bytes 10000000 | tf_op jit(solution)/shard_map/pallas_call | solution.py:459
  82.0 1.8 %copy.16 = bf16[1,40,5120]{2,1,0:T(8,128)(2,1)} copy(bf16[1,40,5120]{2,1,0:T(8,128)(2,1)} %bitcast.6) | data formatting | bytes 819200
